TPU v7x, 32 devices: a whole 2x2x4 slice. The times are simulated.
32 devices in a mesh: groups: 2 (over y), dp: 8 (over z, x), tensor: 2 (over core).
Axes of the slice: x: 2, y: 2, z: 4, core: 2. Of those that a mesh axis runs over, the one named last changes fastest.
Arguments:
- cache_keys: bfloat16 [16, 2048, 1024], P(('groups', 'dp'), None, 'tensor'), parts along dimension 0, may hold values from -32 to 32
- cache_values: bfloat16 [16, 2048, 1024], P(('groups', 'dp'), None, 'tensor'), parts along dimension 0, may hold values from -6 to 6
- lengths: int32 [16], P(('groups', 'dp')), parts along dimension 0, may hold values from 512 to 2048
- parent_scores: float32 [16], P(('groups', 'dp')), parts along dimension 0, may hold values from -6 to 0
- parents: int32 [16], P(('groups', 'dp')), parts along dimension 0, may hold values from 0 to 7, as said below
- queries: bfloat16 [16, 4, 8192], P(('groups', 'dp'), None, 'tensor'), parts along dimension 0, may hold values from -32 to 32
- new_keys: bfloat16 [16, 4, 1024], P(('groups', 'dp'), None, 'tensor'), parts along dimension 0, may hold values from -9 to 9
- new_values: bfloat16 [16, 4, 1024], P(('groups', 'dp'), None, 'tensor'), parts along dimension 0, may hold values from -6 to 6
- reward_weight: bfloat16 [8192], P('tensor'), may hold values from -3 to 3
Outputs:
- attended: bfloat16 [16, 4, 8192], P(('groups', 'dp'), None, 'tensor'), parts along dimension 0
- scores: float32 [16], P(('groups', 'dp')), parts along dimension 0
There are 2 independent parts, one for each index of `groups`. A program takes and returns all parts, laid end to end along the dimension named above; an argument that names none is the same for every part. Nothing has to cross between parts.
Inputs may be any that keep to these rules, and one draw needn't show every extreme that they name: `parents`: each old beam is continued by at most 2 new slots; in every draw some old beams are continued by exactly 2 and others by none.
All inputs are finite; a program needn't handle non-finite values.
Results may differ from a plain program's by a relative error of at most 0.0056.
Values may be sent and summed in bfloat16 or wider, within the bound.
A program may use at most 64 MiB of HBM per device.

v0:
```python
import jax
import jax.numpy as jnp
from jax import lax
from jax.sharding import PartitionSpec as P

HD = 128
CHILDREN = 2


def per_device(
    cache_keys,
    cache_values,
    lengths,
    parent_scores,
    parents,
    queries,
    new_keys,
    new_values,
    reward_weight,
):
    myself = lax.axis_index("dp")
    steps = queries.shape[1]
    width = queries.shape[2]
    heads = width // HD
    kv_heads = cache_keys.shape[2] // HD
    group = heads // kv_heads
    context = cache_keys.shape[1]
    scale = HD ** (-0.5)
    everyone = lax.all_gather(parents, "dp", axis=0, tiled=True)
    slot_ids = jnp.arange(everyone.shape[0])
    earlier = slot_ids[None, :] < slot_ids[:, None]
    same = everyone[None, :] == everyone[:, None]
    rank = jnp.sum((earlier & same).astype(jnp.int32), axis=1)
    mine = everyone == myself
    picker = ((jnp.arange(CHILDREN)[:, None] == rank[None, :]) & mine[None, :]).astype(jnp.bfloat16)
    valid = jnp.arange(context) < lengths[0]
    holder = lax.dynamic_index_in_dim(everyone, myself, 0, keepdims=False)
    own_rank = lax.dynamic_index_in_dim(rank, myself, 0, keepdims=False)
    wanted = holder * CHILDREN + own_rank
    row = queries.reshape(1, steps * width)
    target = (slot_ids == holder)[:, None]
    posted = jnp.where(target, row, jnp.zeros_like(row))
    arrived = lax.all_to_all(posted, "dp", split_axis=0, concat_axis=0, tiled=True)
    gathered = jnp.dot(picker, arrived, preferred_element_type=jnp.float32)
    rows = gathered.astype(jnp.bfloat16).reshape(CHILDREN, steps, width)
    count = rows.shape[0]
    items = rows.shape[1]
    flat = rows.reshape(count * items, kv_heads, group, HD)
    outputs = []
    log_totals = []
    for head in range(kv_heads):
        keys = cache_keys[0, :, head * HD : (head + 1) * HD]
        values = cache_values[0, :, head * HD : (head + 1) * HD]
        logits = (
            jnp.einsum("rjd,cd->rjc", flat[:, head], keys, preferred_element_type=jnp.float32)
            * scale
        )
        logits = jnp.where(valid[None, None, :], logits, -1e30)
        top_here = jnp.max(logits, axis=-1)
        weights = jnp.exp(logits - top_here[..., None])
        total = jnp.sum(weights, axis=-1)
        summed = jnp.einsum(
            "rjc,cd->rjd", weights.astype(jnp.bfloat16), values, preferred_element_type=jnp.float32
        )
        outputs.append(summed / total[..., None])
        log_totals.append(top_here + jnp.log(total))
    parent_out = jnp.stack(outputs, axis=1).reshape(count, items, width).astype(jnp.bfloat16)
    parent_lse = jnp.stack(log_totals, axis=1).reshape(count, items, heads)
    parent_out, parent_lse = (parent_out, parent_lse)
    piece = lax.all_gather(parent_out.reshape(CHILDREN, steps * width), "dp", axis=0, tiled=True)
    hit = (jnp.arange(piece.shape[0]) == wanted).astype(jnp.bfloat16)
    received = jnp.dot(hit[None], piece, preferred_element_type=jnp.float32)
    carried = jnp.broadcast_to(parent_scores[0], (CHILDREN,))
    lse_all, carried_all = (
        lax.all_gather(parent_lse.reshape(CHILDREN, steps * heads), "dp", axis=0, tiled=True),
        lax.all_gather(carried, "dp", axis=0, tiled=True),
    )
    sum_parent = received.reshape(steps, kv_heads, group, HD)
    top_parent = lax.dynamic_index_in_dim(lse_all, wanted, 0, keepdims=False).reshape(
        steps, kv_heads, group
    )
    inherited = lax.dynamic_index_in_dim(carried_all, wanted, 0, keepdims=False)
    query = queries[0].reshape(steps, kv_heads, group, HD)
    own_keys = new_keys[0].reshape(steps, kv_heads, HD)
    own_values = new_values[0].reshape(steps, kv_heads, HD)
    own_logits = (
        jnp.einsum("tgjd,ugd->tgju", query, own_keys, preferred_element_type=jnp.float32) * scale
    )
    causal = jnp.arange(steps)[None, :] <= jnp.arange(steps)[:, None]
    own_logits = jnp.where(causal[:, None, None, :], own_logits, -1e30)
    top_own = jnp.max(own_logits, axis=-1)
    own_weights = jnp.exp(own_logits - top_own[..., None])
    total_own = jnp.sum(own_weights, axis=-1)
    sum_own = jnp.einsum(
        "tgju,ugd->tgjd",
        own_weights.astype(jnp.bfloat16),
        own_values,
        preferred_element_type=jnp.float32,
    )
    top = jnp.maximum(top_parent, top_own)
    factor_parent = jnp.exp(top_parent - top)
    factor_own = jnp.exp(top_own - top)
    merged = (sum_parent * factor_parent[..., None] + sum_own * factor_own[..., None]) / (
        factor_parent + total_own * factor_own
    )[..., None]
    output = merged.reshape(steps, width).astype(jnp.bfloat16)
    partial_reward = jnp.dot(output, reward_weight, preferred_element_type=jnp.float32)
    reward = lax.psum(partial_reward, "tensor")
    score = inherited + jnp.sum(jax.nn.log_sigmoid(reward))
    return (output[None], score.reshape(1))


def solution(mesh):
    return jax.shard_map(
        per_device,
        mesh=mesh,
        in_specs=(
            P(("groups", "dp"), None, "tensor"),
            P(("groups", "dp"), None, "tensor"),
            P(("groups", "dp")),
            P(("groups", "dp")),
            P(("groups", "dp")),
            P(("groups", "dp"), None, "tensor"),
            P(("groups", "dp"), None, "tensor"),
            P(("groups", "dp"), None, "tensor"),
            P("tensor"),
        ),
        out_specs=(P(("groups", "dp"), None, "tensor"), P(("groups", "dp"))),
        check_vma=False,
    )
```

profile of v0, /device:TPU:0, one launch (start us, length us, event | category | flops | bytes accessed | tf_op | source)
XLA Modules:
  0.0 112.8 jit_solution(6933471805586509177)
XLA Ops:
  1.5 1.2 %dynamic-slice = u32[1]{0:T(128)} dynamic-slice(u32[32]{0:T(128)} %constant.50, u32[]{:T(128)S(6)} %add.101), dynamic_slice_sizes={1} | dynamic-slice | bytes 12
  2.7 0.8 dynamic-update-slice
  3.5 13.1 %all-reduce = s32[8]{0:T(128)S(1)} all-reduce(s32[8]{0:T(128)S(1)} %dynamic-update-slice), channel_id=1, replica_groups=mesh['groups'=2,'dp'=8,'tensor'=2] {'dp'}, use_global_device_ids=true, to_apply=%add | all-reduce | flops 8 | bytes 64
  16.5 0.6 dynamic_slice.15
  17.1 0.6 iota_compare_fusion.3
  17.8 0.8 copy.73
  18.6 0.5 broadcast_select_fusion
  19.0 0.6 broadcast.91
  19.6 2.3 %reduce.4 = bf16[8,16384]{1,0:T(8,128)(2,1)S(1)} reduce(bf16[8,1,16384]{2,1,0:T(2,128)(2,1)S(1)} %broadcast_select_fusion, bf16[]{:T(256)} %broadcast.91), dimensions={1}, to_apply=%broadcast_select_fusion.reduce_sub_computation | reduce | bytes 524290 | tf_op jit(solution)/shard_map/jit(_where)/select_n | solution.py:42
  22.0 0.9 reshape.255
  22.8 3.4 %all-to-all-start = ((bf16[8,2,8192]{2,1,0:T(2,128)(2,1)}), bf16[8,2,8192]{2,1,0:T(2,128)(2,1)S(1)}, u32[]{:S(2)}, u32[]{:S(2)}) async-start(bf16[8,2,8192]{2,1,0:T(2,128)(2,1)} %reshape.255), calls=%async_computation | async-start | bytes 524288 | tf_op jit(solution)/shard_map/all_to_all | solution.py:43
  28.1 21.8 %all-reduce.1 = f32[16]{0:T(128)S(1)} all-reduce(f32[16]{0:T(128)S(1)} %broadcast_dynamic-update-slice_fusion), channel_id=1, replica_groups=mesh['groups'=2,'dp'=8,'tensor'=2] {'dp'}, use_global_device_ids=true, to_apply=%add.1 | all-reduce | flops 16 | bytes 128
  51.2 0.6 dynamic_slice.16
  52.4 0.6 dynamic_slice.18
  53.4 0.4 convolution_convert_fusion
  53.9 0.4 fusion.76
  54.3 0.4 fusion.77
  55.1 0.4 fusion.79
  57.8 31.2 %all-gather = bf16[8,2,16384]{2,1,0:T(2,128)(2,1)S(1)} all-gather(bf16[1,2,16384]{2,1,0:T(2,128)(2,1)S(1)} %reshape.224), channel_id=1, replica_groups=mesh['groups'=2,'dp'=8,'tensor'=2] {'dp'}, dimensions={0}, use_global_device_ids=true | all-gather | bytes 589824 | tf_op jit(solution)/shard_map/all_gather | solution.py:70
  89.3 0.4 fusion.26
  89.9 16.4 %all-gather.1 = f32[8,2,128]{2,1,0:T(2,128)S(1)} all-gather(f32[1,2,128]{2,1,0:T(2,128)S(1)} %reshape.226), channel_id=1, replica_groups=mesh['groups'=2,'dp'=8,'tensor'=2] {'dp'}, dimensions={0}, use_global_device_ids=true | all-gather | bytes 9216 | tf_op jit(solution)/shard_map/all_gather | solution.py:75
  106.7 0.6 convert_element_type.53
  107.4 2.4 %psum.7 = f32[4]{0:T(128)S(1)} all-reduce(f32[4]{0:T(128)S(1)} %convolution_bitcast_fusion.1), channel_id=1, replica_groups=mesh['groups'=2,'dp'=8,'tensor'=2] {'tensor'}, use_global_device_ids=true, to_apply=%region_11.12 | all-reduce | flops 4 | bytes 32 | tf_op jit(solution)/shard_map/psum | solution.py:108
  109.8 0.6 fusion.70
  (50 shorter events, 4.5 us)
Async XLA Ops:
  0.6 105.7 %copy-start = (bf16[1,4,512]{2,1,0:T(4,128)(2,1)S(1)}, bf16[1,4,512]{2,1,0:T(4,128)(2,1)}, u32[]{:S(2)}) copy-start(bf16[1,4,512]{2,1,0:T(4,128)(2,1)} %param.16) | copy-start | bytes 12292
  0.6 26.9 %copy-start.3 = (bf16[1,4,4096]{2,1,0:T(4,128)(2,1)S(1)}, bf16[1,4,4096]{2,1,0:T(4,128)(2,1)}, u32[]{:S(2)}) copy-start(bf16[1,4,4096]{2,1,0:T(4,128)(2,1)} %param.14) | copy-start | bytes 98308
  0.7 26.9 %copy-start.5 = (bf16[1,4,512]{2,1,0:T(4,128)(2,1)S(1)}, bf16[1,4,512]{2,1,0:T(4,128)(2,1)}, u32[]{:S(2)}) copy-start(bf16[1,4,512]{2,1,0:T(4,128)(2,1)} %param.15) | copy-start | bytes 12292
  0.7 51.7 %copy-start.4 = (bf16[4096]{0:T(1024)(128)(2,1)S(1)}, bf16[4096]{0:T(1024)(128)(2,1)}, u32[]{:S(2)}) copy-start(bf16[4096]{0:T(1024)(128)(2,1)} %param.17) | copy-start | bytes 24580
  0.7 53.2 %copy-start.1 = (bf16[1,2048,512]{2,1,0:T(8,128)(2,1)S(1)}, bf16[1,2048,512]{2,1,0:T(8,128)(2,1)}, u32[]{:S(2)}) copy-start(bf16[1,2048,512]{2,1,0:T(8,128)(2,1)} %param.9) | copy-start | bytes 6291460
  22.8 30.3 %all-to-all-start = ((bf16[8,2,8192]{2,1,0:T(2,128)(2,1)}), bf16[8,2,8192]{2,1,0:T(2,128)(2,1)S(1)}, u32[]{:S(2)}, u32[]{:S(2)}) async-start(bf16[8,2,8192]{2,1,0:T(2,128)(2,1)} %reshape.255), calls=%async_computation | async-start | bytes 524288 | tf_op jit(solution)/shard_map/all_to_all | solution.py:43
  54.3 1.6 %copy-start.2 = (bf16[1,2048,512]{2,1,0:T(8,128)(2,1)S(1)}, bf16[1,2048,512]{2,1,0:T(8,128)(2,1)}, u32[]{:S(2)}) copy-start(bf16[1,2048,512]{2,1,0:T(8,128)(2,1)} %param.10) | copy-start | bytes 6291460
where the time goes:
time: 113 us
  blocking collectives  84.8 us (75%)
  local copies, waits for them, and re-layouts  7.88 us (7%)
  between operations  7.38 us (7%)
  other arithmetic  5.29 us (5%)
  matrix products  4.04 us (4%)
  starting transfers between devices  3.41 us (3%)
    unnamed x2, blocking collectives  34.8 us
    all_gather x1, blocking collectives, per_device(): lax.all_gather(parent_out.reshape(CHILDREN, steps * width), 'dp', axis=0,...  31.2 us
    all_gather x1, blocking collectives, per_device(): lax.all_gather(parent_lse.reshape(CHILDREN, steps * heads), 'dp', axis=0,...  16.4 us
    unnamed x25, local copies, waits for them, and re-layouts  4.62 us
    all_to_all x1, starting transfers between devices, per_device(): lax.all_to_all(posted, 'dp', split_axis=0, concat_axis=0, tiled=True)  3.41 us
    select_n x2, other arithmetic, per_device(): posted = jnp.where(target, row, jnp.zeros_like(row))  2.8 us
    psum x1, blocking collectives, per_device(): reward = lax.psum(partial_reward, 'tensor')  2.44 us
  transfers between devices with their start and end apart: 1, of which 0 were waited for; matrix products, arithmetic and copies ran while one was open for 2% of the time, Pallas kernels for 0%

commit v1 on v0

v1 whole, which is shorter than its diff:
```python
import functools
import math

import jax
import jax.numpy as jnp
from jax import lax
from jax.experimental import pallas as pl
from jax.experimental.pallas import tpu as pltpu
from jax.sharding import PartitionSpec as P

HD = 128
MESH = pl.DeviceIdType.MESH
F32 = jnp.float32
BF16 = jnp.bfloat16


def kernel(
    n,
    lengths,
    parent_scores,
    parents,
    queries,
    new_keys,
    new_values,
    reward_weight,
    cache_keys,
    cache_values,
    attended,
    scores,
    keys,
    values,
    stage,
    weight,
    ids,
    asked,
    answer,
    answer_lse,
    got,
    got_lse,
    part,
    cache_sems,
    id_sems,
    ask_sems,
    got_sems,
    lse_sems,
    part_sems,
):
    me = lax.axis_index("dp")
    core = lax.axis_index("tensor")
    steps = queries.shape[1]
    heads = queries.shape[2] // HD
    context = cache_keys.shape[1]
    kv_heads = cache_keys.shape[2] // HD
    group = heads // kv_heads
    rows = group * steps
    total_rows = heads * steps
    scale = HD ** (-0.5)
    base2 = scale * math.log2(math.e)

    copy_keys = pltpu.make_async_copy(cache_keys.at[0], keys, cache_sems.at[0])
    copy_values = pltpu.make_async_copy(cache_values.at[0], values, cache_sems.at[1])
    copy_keys.start()
    copy_values.start()

    barrier = pltpu.get_barrier_semaphore()

    def peer(k):
        return lax.rem(me + 1 + k, n)

    def greet(k, carry):
        pl.semaphore_signal(barrier, inc=1, device_id={"dp": peer(k)}, device_id_type=MESH)
        return carry

    lax.fori_loop(0, n - 1, greet, 0)
    pl.semaphore_signal(barrier, inc=1, device_id={"tensor": 1 - core}, device_id_type=MESH)

    for head in range(heads):
        stage[head * steps : (head + 1) * steps, :] = queries[
            0, :, head * HD : (head + 1) * HD
        ].astype(F32)
        weight[head * steps : (head + 1) * steps, :] = jnp.broadcast_to(
            reward_weight[:, head * HD : (head + 1) * HD].astype(F32), (steps, HD)
        )
    query = stage[...].astype(BF16)
    asked[me] = query
    ids[me] = jnp.full((8, HD), parents[0], jnp.int32)

    pl.semaphore_wait(barrier, n)

    def ask_copy(slot, to):
        return pltpu.make_async_remote_copy(
            src_ref=asked.at[slot],
            dst_ref=asked.at[slot],
            send_sem=ask_sems.at[0, to],
            recv_sem=ask_sems.at[1, slot],
            device_id={"dp": to},
            device_id_type=MESH,
        )

    def id_copy(slot, to):
        return pltpu.make_async_remote_copy(
            src_ref=ids.at[slot],
            dst_ref=ids.at[slot],
            send_sem=id_sems.at[0, to],
            recv_sem=id_sems.at[1, slot],
            device_id={"dp": to},
            device_id_type=MESH,
        )

    def got_copy(slot, to):
        return pltpu.make_async_remote_copy(
            src_ref=answer.at[to],
            dst_ref=got.at[slot],
            send_sem=got_sems.at[0, to],
            recv_sem=got_sems.at[1, slot],
            device_id={"dp": to},
            device_id_type=MESH,
        )

    def lse_copy(slot, to):
        return pltpu.make_async_remote_copy(
            src_ref=answer_lse.at[to],
            dst_ref=got_lse.at[slot],
            send_sem=lse_sems.at[0, to],
            recv_sem=lse_sems.at[1, slot],
            device_id={"dp": to},
            device_id_type=MESH,
        )

    def ask(k, carry):
        id_copy(me, peer(k)).start()
        ask_copy(me, peer(k)).start()
        return carry

    lax.fori_loop(0, n - 1, ask, 0)

    own_keys = new_keys[0]
    own_values = new_values[0]
    row_step = lax.rem(lax.broadcasted_iota(jnp.int32, (rows, steps), 0), steps)
    causal = lax.broadcasted_iota(jnp.int32, (rows, steps), 1) <= row_step
    own_sums, own_tops, own_totals = [], [], []
    for head in range(kv_heads):
        q = query[head * rows : (head + 1) * rows]
        logits = lax.dot_general(
            q,
            own_keys[:, head * HD : (head + 1) * HD],
            (((1,), (1,)), ((), ())),
            preferred_element_type=F32,
        )
        logits = jnp.where(causal, logits * scale, -1e30)
        top = jnp.max(logits, axis=1, keepdims=True)
        weights = jnp.exp(logits - top)
        own_tops.append(top)
        own_totals.append(jnp.sum(weights, axis=1, keepdims=True))
        own_sums.append(
            jnp.dot(
                weights.astype(BF16),
                own_values[:, head * HD : (head + 1) * HD],
                preferred_element_type=F32,
            )
        )
    top_own = jnp.concatenate(own_tops, axis=0)
    total_own = jnp.concatenate(own_totals, axis=0)
    sum_own = jnp.concatenate(own_sums, axis=0)

    copy_keys.wait()
    copy_values.wait()

    def asked_wait(k, carry):
        id_copy(peer(k), me).wait_recv()
        ask_copy(peer(k), me).wait_recv()
        return carry

    lax.fori_loop(0, n - 1, asked_wait, 0)

    def find(slot, carry):
        first, last = carry
        mine = ids[slot] == me
        return (
            jnp.minimum(first, jnp.where(mine, slot, n)),
            jnp.maximum(last, jnp.where(mine, slot, -1)),
        )

    first, last = lax.fori_loop(
        0, n, find, (jnp.full((8, HD), n, jnp.int32), jnp.full((8, HD), -1, jnp.int32))
    )
    first = jnp.minimum(jnp.max(first), n - 1)
    last = jnp.maximum(jnp.max(last), 0)
    both = (asked[first], asked[last])

    valid = lax.broadcasted_iota(jnp.int32, (2 * rows, context), 1) < lengths[0]
    outs, lses = ([], []), ([], [])
    for head in range(kv_heads):
        q = jnp.concatenate([b[head * rows : (head + 1) * rows] for b in both], axis=0)
        logits = lax.dot_general(
            q,
            keys[:, head * HD : (head + 1) * HD],
            (((1,), (1,)), ((), ())),
            preferred_element_type=F32,
        )
        logits = jnp.where(valid, logits, -1e30)
        top = jnp.max(logits, axis=1, keepdims=True)
        weights = jnp.exp2((logits - top) * base2)
        total = jnp.sum(weights, axis=1, keepdims=True)
        summed = jnp.dot(
            weights.astype(BF16),
            values[:, head * HD : (head + 1) * HD],
            preferred_element_type=F32,
        )
        out = (summed / total).astype(BF16)
        lse = top * scale + jnp.log(total)
        for child in range(2):
            outs[child].append(out[child * rows : (child + 1) * rows])
            lses[child].append(lse[child * rows : (child + 1) * rows])

    eye = lax.broadcasted_iota(jnp.int32, (total_rows, total_rows), 0) == lax.broadcasted_iota(
        jnp.int32, (total_rows, total_rows), 1
    )
    out_by_child = [jnp.concatenate(o, axis=0) for o in outs]
    lse_by_child = [
        jnp.sum(jnp.where(eye, jnp.concatenate(l, axis=0), 0.0), axis=0, keepdims=True)
        for l in lses
    ]
    score_row = jnp.full((1, total_rows), parent_scores[0], F32)

    def reply(k, carry):
        to = peer(k)
        answer[to] = jnp.where(to == first, out_by_child[0], out_by_child[1])
        answer_lse[to, 0:1, :] = jnp.where(to == first, lse_by_child[0], lse_by_child[1])
        answer_lse[to, 1:2, :] = score_row
        got_copy(me, to).start()
        lse_copy(me, to).start()
        return carry

    lax.fori_loop(0, n - 1, reply, 0)
    got[me] = jnp.where(me == first, out_by_child[0], out_by_child[1])
    got_lse[me, 0:1, :] = jnp.where(me == first, lse_by_child[0], lse_by_child[1])
    got_lse[me, 1:2, :] = score_row

    def reply_wait(k, carry):
        got_copy(peer(k), me).wait_recv()
        lse_copy(peer(k), me).wait_recv()
        return carry

    lax.fori_loop(0, n - 1, reply_wait, 0)

    holder = parents[0]
    parent_out = got[holder].astype(F32)
    lse_rows = got_lse[holder]
    inherited = jnp.max(lse_rows[1:2, :])
    parent_lse = jnp.sum(jnp.where(eye, lse_rows[0:1, :], 0.0), axis=1, keepdims=True)
    top = jnp.maximum(parent_lse, top_own)
    factor_parent = jnp.exp(parent_lse - top)
    factor_own = jnp.exp(top_own - top)
    merged = (parent_out * factor_parent + sum_own * factor_own) / (
        factor_parent + total_own * factor_own
    )
    output = merged.astype(BF16).astype(F32)
    stage[...] = output
    product = output * weight[...]
    tall = 2 * steps
    partial = product[0:tall]
    for i in range(1, total_rows // tall):
        partial = partial + product[i * tall : (i + 1) * tall]
    part[0] = partial
    part_copy = pltpu.make_async_remote_copy(
        src_ref=part.at[0],
        dst_ref=part.at[1],
        send_sem=part_sems.at[0],
        recv_sem=part_sems.at[1],
        device_id={"tensor": 1 - core},
        device_id_type=MESH,
    )
    part_copy.start()
    for head in range(heads):
        attended[0, :, head * HD : (head + 1) * HD] = stage[
            head * steps : (head + 1) * steps, :
        ].astype(BF16)

    def sent_wait(k, carry):
        id_copy(me, peer(k)).wait_send()
        ask_copy(me, peer(k)).wait_send()
        got_copy(me, peer(k)).wait_send()
        lse_copy(me, peer(k)).wait_send()
        return carry

    lax.fori_loop(0, n - 1, sent_wait, 0)
    part_copy.wait()
    reward = jnp.sum(part[0] + part[1], axis=1, keepdims=True)
    reward = reward[0:steps] + reward[steps : 2 * steps]
    logs = jnp.minimum(reward, 0.0) - jnp.log1p(jnp.exp(-jnp.abs(reward)))
    scores[0] = inherited + jnp.sum(logs)


def per_device(
    n,
    cache_keys,
    cache_values,
    lengths,
    parent_scores,
    parents,
    queries,
    new_keys,
    new_values,
    reward_weight,
):
    steps = queries.shape[1]
    width = queries.shape[2]
    context, kv_width = cache_keys.shape[1:]
    total_rows = steps * width // HD
    vmem = pl.BlockSpec(memory_space=pltpu.VMEM)
    smem = pl.BlockSpec(memory_space=pltpu.SMEM)
    hbm = pl.BlockSpec(memory_space=pl.ANY)
    return pl.pallas_call(
        functools.partial(kernel, n),
        out_shape=(
            jax.ShapeDtypeStruct(queries.shape, BF16),
            jax.ShapeDtypeStruct((1,), F32),
        ),
        in_specs=[smem] * 3 + [vmem] * 4 + [hbm] * 2,
        out_specs=(vmem, smem),
        scratch_shapes=[
            pltpu.VMEM((context, kv_width), BF16),
            pltpu.VMEM((context, kv_width), BF16),
            pltpu.VMEM((total_rows, HD), F32),
            pltpu.VMEM((total_rows, HD), F32),
            pltpu.VMEM((n, 8, HD), jnp.int32),
            pltpu.VMEM((n, total_rows, HD), BF16),
            pltpu.VMEM((n, total_rows, HD), BF16),
            pltpu.VMEM((n, 8, total_rows), F32),
            pltpu.VMEM((n, total_rows, HD), BF16),
            pltpu.VMEM((n, 8, total_rows), F32),
            pltpu.VMEM((2, 2 * steps, HD), F32),
            pltpu.SemaphoreType.DMA((2,)),
            pltpu.SemaphoreType.DMA((2, n)),
            pltpu.SemaphoreType.DMA((2, n)),
            pltpu.SemaphoreType.DMA((2, n)),
            pltpu.SemaphoreType.DMA((2, n)),
            pltpu.SemaphoreType.DMA((2,)),
        ],
        compiler_params=pltpu.CompilerParams(
            collective_id=0, has_side_effects=True, vmem_limit_bytes=48 * 1024 * 1024
        ),
    )(
        lengths,
        parent_scores,
        parents,
        queries,
        new_keys,
        new_values,
        reward_weight.reshape(1, width),
        cache_keys,
        cache_values,
    )


def solution(mesh):
    beams = P(("groups", "dp"))
    split = P(("groups", "dp"), None, "tensor")
    return jax.shard_map(
        functools.partial(per_device, mesh.shape["dp"]),
        mesh=mesh,
        in_specs=(split, split, beams, beams, beams, split, split, split, P("tensor")),
        out_specs=(split, beams),
        check_vma=False,
    )
```

time: 113 us -> 35.6 us (0.32)
  the two profiles are of different devices: /device:TPU:0 before, /device:TPU:25 now
where the time goes in v1:
time: 35.6 us; the launch traced here: 35.2 us
  Pallas kernels  24.3 us (68%)
  local copies, waits for them, and re-layouts  6.63 us (19%)
  between operations  4.28 us (12%)
    pallas_call x1, Pallas kernels, per_device(): pl.pallas_call(functools.partial(kernel, n), out_shape=(jax.ShapeDtypeStr...  24.3 us
    unnamed x11, local copies, waits for them, and re-layouts  5.92 us

profile of v1, /device:TPU:25, one launch (start us, length us, event | category | flops | bytes accessed | tf_op | source)
XLA Modules:
  0.0 35.2 jit_solution(17249704572199335877)
XLA Ops:
  2.6 0.7 %reshape.7.reward_weight = bf16[1,4096]{1,0:T(2,128)(2,1)S(1)} reshape(bf16[4096]{0:T(1024)(128)(2,1)} %param.17) | data formatting | bytes 16384 | tf_op jit(solution)/shard_map/reshape | solution.py:351
  3.3 0.0 copy-start
  3.3 1.6 %copy-done = bf16[1,2048,512]{2,1,0:T(8,128)(2,1)S(1)} copy-done((bf16[1,2048,512]{2,1,0:T(8,128)(2,1)S(1)}, bf16[1,2048,512]{2,1,0:T(8,128)(2,1)}, u32[]{:S(2)}) %copy-start) | copy-done | bytes 2097176
  4.9 0.0 copy-start.1
  4.9 1.6 %copy-done.1 = bf16[1,2048,512]{2,1,0:T(8,128)(2,1)S(1)} copy-done((bf16[1,2048,512]{2,1,0:T(8,128)(2,1)S(1)}, bf16[1,2048,512]{2,1,0:T(8,128)(2,1)}, u32[]{:S(2)}) %copy-start.1) | copy-done | bytes 2097176
  6.5 0.0 copy-start.2
  6.5 0.8 %copy-done.2 = bf16[1,4,4096]{2,1,0:T(4,128)(2,1)S(1)} copy-done((bf16[1,4,4096]{2,1,0:T(4,128)(2,1)S(1)}, bf16[1,4,4096]{2,1,0:T(4,128)(2,1)}, u32[]{:S(2)}) %copy-start.2) | copy-done | bytes 32792
  7.2 0.0 copy-start.3
  7.2 0.7 %copy-done.3 = bf16[1,4,512]{2,1,0:T(4,128)(2,1)S(1)} copy-done((bf16[1,4,512]{2,1,0:T(4,128)(2,1)S(1)}, bf16[1,4,512]{2,1,0:T(4,128)(2,1)}, u32[]{:S(2)}) %copy-start.3) | copy-done | bytes 4120
  7.9 0.0 copy-start.4
  7.9 0.7 %copy-done.4 = bf16[1,4,512]{2,1,0:T(4,128)(2,1)S(1)} copy-done((bf16[1,4,512]{2,1,0:T(4,128)(2,1)S(1)}, bf16[1,4,512]{2,1,0:T(4,128)(2,1)}, u32[]{:S(2)}) %copy-start.4) | copy-done | bytes 4120
  8.6 24.3 %shard_map.104 = (bf16[1,4,4096]{2,1,0:T(4,128)(2,1)S(1)}, f32[1]{0:T(128)}) custom-call(s32[1]{0:T(128)S(6)} %copy.13.lengths, f32[1]{0:T(128)S(6)} %copy.14.parent_scores, s32[1]{0:T(128)S(6)} %copy.15.parents, bf16[1,4,4096]{2,1,0:T(4,128)(2,1)S(1)} %copy-done.2, bf16[1,4,512]{2,1,0:T(4,128)(2,1)S(1)} %copy-done.3, bf16[1,4,512]{2,1,0:T(4,128)(2,1)S(1)} %copy-done.4, ...), custom_call_target="tpu_custom_call" | custom-call | tf_op jit(solution)/shard_map/pallas_call | solution.py:314
  32.9 0.6 %copy.16 = bf16[1,4,4096]{2,1,0:T(4,128)(2,1)} copy(bf16[1,4,4096]{2,1,0:T(4,128)(2,1)S(1)} %get-tuple-element.4) | data formatting | bytes 65536
Async XLA Ops:
  3.3 1.6 %copy-start = (bf16[1,2048,512]{2,1,0:T(8,128)(2,1)S(1)}, bf16[1,2048,512]{2,1,0:T(8,128)(2,1)}, u32[]{:S(2)}) copy-start(bf16[1,2048,512]{2,1,0:T(8,128)(2,1)} %cache_keys.1) | copy-start | bytes 6291460
  4.9 1.6 %copy-start.1 = (bf16[1,2048,512]{2,1,0:T(8,128)(2,1)S(1)}, bf16[1,2048,512]{2,1,0:T(8,128)(2,1)}, u32[]{:S(2)}) copy-start(bf16[1,2048,512]{2,1,0:T(8,128)(2,1)} %cache_values.1) | copy-start | bytes 6291460
  6.5 0.8 %copy-start.2 = (bf16[1,4,4096]{2,1,0:T(4,128)(2,1)S(1)}, bf16[1,4,4096]{2,1,0:T(4,128)(2,1)}, u32[]{:S(2)}) copy-start(bf16[1,4,4096]{2,1,0:T(4,128)(2,1)} %queries.1) | copy-start | bytes 98308
  7.2 0.7 %copy-start.3 = (bf16[1,4,512]{2,1,0:T(4,128)(2,1)S(1)}, bf16[1,4,512]{2,1,0:T(4,128)(2,1)}, u32[]{:S(2)}) copy-start(bf16[1,4,512]{2,1,0:T(4,128)(2,1)} %new_keys.1) | copy-start | bytes 12292
  7.9 0.7 %copy-start.4 = (bf16[1,4,512]{2,1,0:T(4,128)(2,1)S(1)}, bf16[1,4,512]{2,1,0:T(4,128)(2,1)}, u32[]{:S(2)}) copy-start(bf16[1,4,512]{2,1,0:T(4,128)(2,1)} %new_values.1) | copy-start | bytes 12292

commit v2 on v1

--- a/solution.py
+++ b/solution.py
@@ -16,6 +16,17 @@
 
 def kernel(
     n,
+    lengths_in,
+    parent_scores_in,
+    parents_in,
+    queries_in,
+    new_keys_in,
+    new_values_in,
+    reward_weight_in,
+    cache_keys,
+    cache_values,
+    attended,
+    scores,
     lengths,
     parent_scores,
     parents,
@@ -23,10 +34,6 @@
     new_keys,
     new_values,
     reward_weight,
-    cache_keys,
-    cache_values,
-    attended,
-    scores,
     keys,
     values,
     stage,
@@ -38,6 +45,7 @@
     got,
     got_lse,
     part,
+    small_sems,
     cache_sems,
     id_sems,
     ask_sems,
@@ -57,6 +65,22 @@
     scale = HD ** (-0.5)
     base2 = scale * math.log2(math.e)
 
+    small = [
+        pltpu.make_async_copy(source, target, small_sems.at[i])
+        for i, (source, target) in enumerate(
+            (
+                (queries_in, queries),
+                (parents_in, parents),
+                (new_keys_in, new_keys),
+                (new_values_in, new_values),
+                (reward_weight_in, reward_weight),
+                (lengths_in, lengths),
+                (parent_scores_in, parent_scores),
+            )
+        )
+    ]
+    for copy in small:
+        copy.start()
     copy_keys = pltpu.make_async_copy(cache_keys.at[0], keys, cache_sems.at[0])
     copy_values = pltpu.make_async_copy(cache_values.at[0], values, cache_sems.at[1])
     copy_keys.start()
@@ -74,13 +98,12 @@
     lax.fori_loop(0, n - 1, greet, 0)
     pl.semaphore_signal(barrier, inc=1, device_id={"tensor": 1 - core}, device_id_type=MESH)
 
+    small[0].wait()
+    small[1].wait()
     for head in range(heads):
         stage[head * steps : (head + 1) * steps, :] = queries[
             0, :, head * HD : (head + 1) * HD
         ].astype(F32)
-        weight[head * steps : (head + 1) * steps, :] = jnp.broadcast_to(
-            reward_weight[:, head * HD : (head + 1) * HD].astype(F32), (steps, HD)
-        )
     query = stage[...].astype(BF16)
     asked[me] = query
     ids[me] = jnp.full((8, HD), parents[0], jnp.int32)
@@ -133,6 +156,13 @@
         return carry
 
     lax.fori_loop(0, n - 1, ask, 0)
+
+    for copy in small[2:]:
+        copy.wait()
+    for head in range(heads):
+        weight[head * steps : (head + 1) * steps, :] = jnp.broadcast_to(
+            reward_weight[head * HD : (head + 1) * HD].astype(F32)[None], (steps, HD)
+        )
 
     own_keys = new_keys[0]
     own_values = new_values[0]
@@ -188,7 +218,8 @@
     last = jnp.maximum(jnp.max(last), 0)
     both = (asked[first], asked[last])
 
-    valid = lax.broadcasted_iota(jnp.int32, (2 * rows, context), 1) < lengths[0]
+    place = lax.broadcasted_iota(jnp.int32, (1, context), 1)
+    bias = jnp.where(place < lengths[0], 0.0, -1e30)
     outs, lses = ([], []), ([], [])
     for head in range(kv_heads):
         q = jnp.concatenate([b[head * rows : (head + 1) * rows] for b in both], axis=0)
@@ -198,7 +229,7 @@
             (((1,), (1,)), ((), ())),
             preferred_element_type=F32,
         )
-        logits = jnp.where(valid, logits, -1e30)
+        logits = logits + bias
         top = jnp.max(logits, axis=1, keepdims=True)
         weights = jnp.exp2((logits - top) * base2)
         total = jnp.sum(weights, axis=1, keepdims=True)
@@ -310,16 +341,22 @@
     total_rows = steps * width // HD
     vmem = pl.BlockSpec(memory_space=pltpu.VMEM)
     smem = pl.BlockSpec(memory_space=pltpu.SMEM)
-    hbm = pl.BlockSpec(memory_space=pl.ANY)
     return pl.pallas_call(
         functools.partial(kernel, n),
         out_shape=(
             jax.ShapeDtypeStruct(queries.shape, BF16),
             jax.ShapeDtypeStruct((1,), F32),
         ),
-        in_specs=[smem] * 3 + [vmem] * 4 + [hbm] * 2,
+        in_specs=[pl.BlockSpec(memory_space=pltpu.HBM)] * 9,
         out_specs=(vmem, smem),
         scratch_shapes=[
+            pltpu.SMEM((1,), jnp.int32),
+            pltpu.SMEM((1,), F32),
+            pltpu.SMEM((1,), jnp.int32),
+            pltpu.VMEM(queries.shape, BF16),
+            pltpu.VMEM(new_keys.shape, BF16),
+            pltpu.VMEM(new_values.shape, BF16),
+            pltpu.VMEM(reward_weight.shape, BF16),
             pltpu.VMEM((context, kv_width), BF16),
             pltpu.VMEM((context, kv_width), BF16),
             pltpu.VMEM((total_rows, HD), F32),
@@ -331,6 +368,7 @@
             pltpu.VMEM((n, total_rows, HD), BF16),
             pltpu.VMEM((n, 8, total_rows), F32),
             pltpu.VMEM((2, 2 * steps, HD), F32),
+            pltpu.SemaphoreType.DMA((7,)),
             pltpu.SemaphoreType.DMA((2,)),
             pltpu.SemaphoreType.DMA((2, n)),
             pltpu.SemaphoreType.DMA((2, n)),
@@ -339,7 +377,7 @@
             pltpu.SemaphoreType.DMA((2,)),
         ],
         compiler_params=pltpu.CompilerParams(
-            collective_id=0, has_side_effects=True, vmem_limit_bytes=48 * 1024 * 1024
+            collective_id=0, has_side_effects=True, vmem_limit_bytes=63 * 1024 * 1024
         ),
     )(
         lengths,
@@ -348,7 +386,7 @@
         queries,
         new_keys,
         new_values,
-        reward_weight.reshape(1, width),
+        reward_weight,
         cache_keys,
         cache_values,
     )

time: 35.6 us -> 30.1 us (0.85)
  the two profiles are of different devices: /device:TPU:25 before, /device:TPU:29 now
where the time goes in v2:
time: 30.1 us; the launch traced here: 29.9 us
  Pallas kernels  24.2 us (80%)
  between operations  4.34 us (14%)
  local copies, waits for them, and re-layouts  1.39 us (5%)
    pallas_call x1, Pallas kernels, per_device(): pl.pallas_call(functools.partial(kernel, n), out_shape=(jax.ShapeDtypeStr...  24.2 us
    unnamed x1, local copies, waits for them, and re-layouts  1.39 us

profile of v2, /device:TPU:29, one launch (start us, length us, event | category | flops | bytes accessed | tf_op | source)
XLA Modules:
  0.0 29.9 jit_solution(13612950783495329339)
XLA Ops:
  2.6 24.2 %shard_map.104 = (bf16[1,4,4096]{2,1,0:T(4,128)(2,1)}, f32[1]{0:T(128)}) custom-call(s32[1]{0:T(128)S(6)} %copy.13.lengths_in, f32[1]{0:T(128)S(6)} %copy.14.parent_scores_in, s32[1]{0:T(128)S(6)} %copy.15.parents_in, bf16[1,4,4096]{2,1,0:T(4,128)(2,1)} %queries_in.1, bf16[1,4,512]{2,1,0:T(4,128)(2,1)} %new_keys_in.1, bf16[1,4,512]{2,1,0:T(4,128)(2,1)} %new_values_in.1, ...), custom_call_target="tpu_custom_call" | custom-call | tf_op jit(solution)/shard_map/pallas_call | solution.py:344
  26.7 1.4 %copy.16 = bf16[1,4,4096]{2,1,0:T(4,128)(2,1)} copy(bf16[1,4,4096]{2,1,0:T(4,128)(2,1)} %get-tuple-element.4) | data formatting | bytes 65536

commit v3 on v2

--- a/solution.py
+++ b/solution.py
@@ -12,6 +12,13 @@
 MESH = pl.DeviceIdType.MESH
 F32 = jnp.float32
 BF16 = jnp.bfloat16
+
+
+def inner_of(n):
+    inner = 1
+    while n % (2 * inner) == 0 and 4 * inner * inner <= n:
+        inner *= 2
+    return inner
 
 
 def kernel(
@@ -42,6 +49,8 @@
     asked,
     answer,
     answer_lse,
+    relay,
+    picked,
     got,
     got_lse,
     part,
@@ -49,11 +58,16 @@
     cache_sems,
     id_sems,
     ask_sems,
+    relay_sems,
     got_sems,
     lse_sems,
     part_sems,
 ):
     me = lax.axis_index("dp")
+    inner = inner_of(n)
+    outer = n // inner
+    z = me // inner
+    x = lax.rem(me, inner)
     core = lax.axis_index("tensor")
     steps = queries.shape[1]
     heads = queries.shape[2] // HD
@@ -110,11 +124,11 @@
 
     pl.semaphore_wait(barrier, n)
 
-    def ask_copy(slot, to):
+    def ask_copy(slot, to, send):
         return pltpu.make_async_remote_copy(
             src_ref=asked.at[slot],
             dst_ref=asked.at[slot],
-            send_sem=ask_sems.at[0, to],
+            send_sem=ask_sems.at[0, send],
             recv_sem=ask_sems.at[1, slot],
             device_id={"dp": to},
             device_id_type=MESH,
@@ -130,13 +144,23 @@
             device_id_type=MESH,
         )
 
-    def got_copy(slot, to):
+    def relay_copy(source, to, far):
         return pltpu.make_async_remote_copy(
-            src_ref=answer.at[to],
-            dst_ref=got.at[slot],
+            src_ref=answer.at[far * inner + to],
+            dst_ref=relay.at[far * inner + source],
+            send_sem=relay_sems.at[0, far * inner + to],
+            recv_sem=relay_sems.at[1, far * inner + source],
+            device_id={"dp": z * inner + to},
+            device_id_type=MESH,
+        )
+
+    def got_copy(source, to):
+        return pltpu.make_async_remote_copy(
+            src_ref=picked.at[to],
+            dst_ref=got.at[source],
             send_sem=got_sems.at[0, to],
-            recv_sem=got_sems.at[1, slot],
-            device_id={"dp": to},
+            recv_sem=got_sems.at[1, source],
+            device_id={"dp": to * inner + x},
             device_id_type=MESH,
         )
 
@@ -150,12 +174,34 @@
             device_id_type=MESH,
         )
 
-    def ask(k, carry):
+    def far(k):
+        return lax.rem(z + 1 + k, outer)
+
+    def near(k):
+        return lax.rem(x + 1 + k, inner)
+
+    def ask_far(k, carry):
+        ask_copy(me, far(k) * inner + x, far(k) * inner + x).start()
+        return carry
+
+    def ask_near(line, start):
+        def body(k, carry):
+            copy = ask_copy(line * inner + x, z * inner + near(k), line * inner + near(k))
+            if start:
+                copy.start()
+            else:
+                copy.wait_send()
+            return carry
+
+        lax.fori_loop(0, inner - 1, body, 0)
+
+    def tell(k, carry):
         id_copy(me, peer(k)).start()
-        ask_copy(me, peer(k)).start()
-        return carry
-
-    lax.fori_loop(0, n - 1, ask, 0)
+        return carry
+
+    lax.fori_loop(0, outer - 1, ask_far, 0)
+    ask_near(z, True)
+    lax.fori_loop(0, n - 1, tell, 0)
 
     for copy in small[2:]:
         copy.wait()
@@ -163,6 +209,14 @@
         weight[head * steps : (head + 1) * steps, :] = jnp.broadcast_to(
             reward_weight[head * HD : (head + 1) * HD].astype(F32)[None], (steps, HD)
         )
+
+    def pass_on(k, carry):
+        line = lax.rem(z + outer - 1 - k, outer)
+        ask_copy(line * inner + x, me, me).wait_recv()
+        ask_near(line, True)
+        return carry
+
+    lax.fori_loop(0, outer - 1, pass_on, 0)
 
     own_keys = new_keys[0]
     own_values = new_values[0]
@@ -198,10 +252,15 @@
 
     def asked_wait(k, carry):
         id_copy(peer(k), me).wait_recv()
-        ask_copy(peer(k), me).wait_recv()
+        return carry
+
+    def passed_wait(k, carry):
+        slot = lax.rem(k, outer) * inner + near(k // outer)
+        ask_copy(slot, me, me).wait_recv()
         return carry
 
     lax.fori_loop(0, n - 1, asked_wait, 0)
+    lax.fori_loop(0, outer * (inner - 1), passed_wait, 0)
 
     def find(slot, carry):
         first, last = carry
@@ -254,29 +313,63 @@
     ]
     score_row = jnp.full((1, total_rows), parent_scores[0], F32)
 
-    def reply(k, carry):
+    def pick(slot):
+        return jnp.where(slot == first, out_by_child[0], out_by_child[1])
+
+    def reply_near(k, carry):
+        line = lax.rem(z + 1 + lax.rem(k, outer), outer)
+        to = near(k // outer)
+        answer[line * inner + to] = pick(line * inner + to)
+        relay_copy(x, to, line).start()
+        return carry
+
+    lax.fori_loop(0, outer * (inner - 1), reply_near, 0)
+
+    def reply_lse(k, carry):
         to = peer(k)
-        answer[to] = jnp.where(to == first, out_by_child[0], out_by_child[1])
         answer_lse[to, 0:1, :] = jnp.where(to == first, lse_by_child[0], lse_by_child[1])
         answer_lse[to, 1:2, :] = score_row
-        got_copy(me, to).start()
         lse_copy(me, to).start()
         return carry
 
-    lax.fori_loop(0, n - 1, reply, 0)
-    got[me] = jnp.where(me == first, out_by_child[0], out_by_child[1])
+    lax.fori_loop(0, n - 1, reply_lse, 0)
     got_lse[me, 0:1, :] = jnp.where(me == first, lse_by_child[0], lse_by_child[1])
     got_lse[me, 1:2, :] = score_row
 
+    def collect(line):
+        slot = line * inner + x
+        parent = jnp.max(ids[slot])
+        row = pick(slot)
+        for k in range(inner - 1):
+            relay_copy(near(k), x, line).wait_recv()
+            row = jnp.where(
+                parent == z * inner + near(k), relay[line * inner + near(k)], row
+            )
+        return row
+
+    def reply_far(k, carry):
+        to = far(k)
+        picked[to] = collect(to)
+        got_copy(z, to).start()
+        return carry
+
+    lax.fori_loop(0, outer - 1, reply_far, 0)
+    got[z] = collect(z)
+
+    def lse_wait(k, carry):
+        lse_copy(peer(k), me).wait_recv()
+        return carry
+
+    lax.fori_loop(0, n - 1, lse_wait, 0)
+
     def reply_wait(k, carry):
-        got_copy(peer(k), me).wait_recv()
-        lse_copy(peer(k), me).wait_recv()
-        return carry
-
-    lax.fori_loop(0, n - 1, reply_wait, 0)
+        got_copy(far(k), z).wait_recv()
+        return carry
+
+    lax.fori_loop(0, outer - 1, reply_wait, 0)
 
     holder = parents[0]
-    parent_out = got[holder].astype(F32)
+    parent_out = got[holder // inner].astype(F32)
     lse_rows = got_lse[holder]
     inherited = jnp.max(lse_rows[1:2, :])
     parent_lse = jnp.sum(jnp.where(eye, lse_rows[0:1, :], 0.0), axis=1, keepdims=True)
@@ -310,12 +403,26 @@
 
     def sent_wait(k, carry):
         id_copy(me, peer(k)).wait_send()
-        ask_copy(me, peer(k)).wait_send()
-        got_copy(me, peer(k)).wait_send()
         lse_copy(me, peer(k)).wait_send()
         return carry
 
+    def far_wait(k, carry):
+        ask_copy(me, far(k) * inner + x, far(k) * inner + x).wait_send()
+        got_copy(z, far(k)).wait_send()
+        return carry
+
+    def near_wait(k, carry):
+        ask_near(k, False)
+        return carry
+
+    def relay_wait(k, carry):
+        relay_copy(x, near(k // outer), lax.rem(k, outer)).wait_send()
+        return carry
+
     lax.fori_loop(0, n - 1, sent_wait, 0)
+    lax.fori_loop(0, outer - 1, far_wait, 0)
+    lax.fori_loop(0, outer, near_wait, 0)
+    lax.fori_loop(0, outer * (inner - 1), relay_wait, 0)
     part_copy.wait()
     reward = jnp.sum(part[0] + part[1], axis=1, keepdims=True)
     reward = reward[0:steps] + reward[steps : 2 * steps]
@@ -366,10 +473,13 @@
             pltpu.VMEM((n, total_rows, HD), BF16),
             pltpu.VMEM((n, 8, total_rows), F32),
             pltpu.VMEM((n, total_rows, HD), BF16),
+            pltpu.VMEM((n // inner_of(n), total_rows, HD), BF16),
+            pltpu.VMEM((n // inner_of(n), total_rows, HD), BF16),
             pltpu.VMEM((n, 8, total_rows), F32),
             pltpu.VMEM((2, 2 * steps, HD), F32),
             pltpu.SemaphoreType.DMA((7,)),
             pltpu.SemaphoreType.DMA((2,)),
+            pltpu.SemaphoreType.DMA((2, n)),
             pltpu.SemaphoreType.DMA((2, n)),
             pltpu.SemaphoreType.DMA((2, n)),
             pltpu.SemaphoreType.DMA((2, n)),

time: 30.1 us -> 31.9 us (1.060)
  the two profiles are of different devices: /device:TPU:29 before, /device:TPU:0 now
where the time goes in v3:
time: 31.9 us; the launch traced here: 31.7 us
  Pallas kernels  26 us (82%)
  between operations  4.34 us (14%)
  local copies, waits for them, and re-layouts  1.39 us (4%)
    pallas_call x1, Pallas kernels, per_device(): pl.pallas_call(functools.partial(kernel, n), out_shape=(jax.ShapeDtypeStr...  26 us
    unnamed x1, local copies, waits for them, and re-layouts  1.39 us

profile of v3, /device:TPU:0, one launch (start us, length us, event | category | flops | bytes accessed | tf_op | source)
XLA Modules:
  0.0 31.7 jit_solution(6611206430479654295)
XLA Ops:
  2.6 26.0 %shard_map.104 = (bf16[1,4,4096]{2,1,0:T(4,128)(2,1)}, f32[1]{0:T(128)}) custom-call(s32[1]{0:T(128)S(6)} %copy.13.lengths_in, f32[1]{0:T(128)S(6)} %copy.14.parent_scores_in, s32[1]{0:T(128)S(6)} %copy.15.parents_in, bf16[1,4,4096]{2,1,0:T(4,128)(2,1)} %queries_in.1, bf16[1,4,512]{2,1,0:T(4,128)(2,1)} %new_keys_in.1, bf16[1,4,512]{2,1,0:T(4,128)(2,1)} %new_values_in.1, ...), custom_call_target="tpu_custom_call" | custom-call | tf_op jit(solution)/shard_map/pallas_call | solution.py:451
  28.6 1.4 %copy.16 = bf16[1,4,4096]{2,1,0:T(4,128)(2,1)} copy(bf16[1,4,4096]{2,1,0:T(4,128)(2,1)} %get-tuple-element.4) | data formatting | bytes 65536

commit v4 on v2

--- a/solution.py
+++ b/solution.py
@@ -12,6 +12,13 @@
 MESH = pl.DeviceIdType.MESH
 F32 = jnp.float32
 BF16 = jnp.bfloat16
+
+
+def inner_of(n):
+    inner = 1
+    while n % (2 * inner) == 0 and 4 * inner * inner <= n:
+        inner *= 2
+    return inner
 
 
 def kernel(
@@ -54,6 +61,10 @@
     part_sems,
 ):
     me = lax.axis_index("dp")
+    inner = inner_of(n)
+    outer = n // inner
+    z = me // inner
+    x = lax.rem(me, inner)
     core = lax.axis_index("tensor")
     steps = queries.shape[1]
     heads = queries.shape[2] // HD
@@ -110,11 +121,11 @@
 
     pl.semaphore_wait(barrier, n)
 
-    def ask_copy(slot, to):
+    def ask_copy(slot, to, send):
         return pltpu.make_async_remote_copy(
             src_ref=asked.at[slot],
             dst_ref=asked.at[slot],
-            send_sem=ask_sems.at[0, to],
+            send_sem=ask_sems.at[0, send],
             recv_sem=ask_sems.at[1, slot],
             device_id={"dp": to},
             device_id_type=MESH,
@@ -150,12 +161,34 @@
             device_id_type=MESH,
         )
 
-    def ask(k, carry):
+    def far(k):
+        return lax.rem(z + 1 + k, outer)
+
+    def near(k):
+        return lax.rem(x + 1 + k, inner)
+
+    def ask_far(k, carry):
+        ask_copy(me, far(k) * inner + x, far(k) * inner + x).start()
+        return carry
+
+    def ask_near(line, start):
+        def body(k, carry):
+            copy = ask_copy(line * inner + x, z * inner + near(k), line * inner + near(k))
+            if start:
+                copy.start()
+            else:
+                copy.wait_send()
+            return carry
+
+        lax.fori_loop(0, inner - 1, body, 0)
+
+    def tell(k, carry):
         id_copy(me, peer(k)).start()
-        ask_copy(me, peer(k)).start()
-        return carry
-
-    lax.fori_loop(0, n - 1, ask, 0)
+        return carry
+
+    lax.fori_loop(0, outer - 1, ask_far, 0)
+    ask_near(z, True)
+    lax.fori_loop(0, n - 1, tell, 0)
 
     for copy in small[2:]:
         copy.wait()
@@ -163,6 +196,14 @@
         weight[head * steps : (head + 1) * steps, :] = jnp.broadcast_to(
             reward_weight[head * HD : (head + 1) * HD].astype(F32)[None], (steps, HD)
         )
+
+    def pass_on(k, carry):
+        line = lax.rem(z + outer - 1 - k, outer)
+        ask_copy(line * inner + x, me, me).wait_recv()
+        ask_near(line, True)
+        return carry
+
+    lax.fori_loop(0, outer - 1, pass_on, 0)
 
     own_keys = new_keys[0]
     own_values = new_values[0]
@@ -198,10 +239,15 @@
 
     def asked_wait(k, carry):
         id_copy(peer(k), me).wait_recv()
-        ask_copy(peer(k), me).wait_recv()
+        return carry
+
+    def passed_wait(k, carry):
+        slot = lax.rem(k, outer) * inner + near(k // outer)
+        ask_copy(slot, me, me).wait_recv()
         return carry
 
     lax.fori_loop(0, n - 1, asked_wait, 0)
+    lax.fori_loop(0, outer * (inner - 1), passed_wait, 0)
 
     def find(slot, carry):
         first, last = carry
@@ -310,12 +356,21 @@
 
     def sent_wait(k, carry):
         id_copy(me, peer(k)).wait_send()
-        ask_copy(me, peer(k)).wait_send()
+        lse_copy(me, peer(k)).wait_send()
         got_copy(me, peer(k)).wait_send()
-        lse_copy(me, peer(k)).wait_send()
+        return carry
+
+    def far_wait(k, carry):
+        ask_copy(me, far(k) * inner + x, far(k) * inner + x).wait_send()
+        return carry
+
+    def near_wait(k, carry):
+        ask_near(k, False)
         return carry
 
     lax.fori_loop(0, n - 1, sent_wait, 0)
+    lax.fori_loop(0, outer - 1, far_wait, 0)
+    lax.fori_loop(0, outer, near_wait, 0)
     part_copy.wait()
     reward = jnp.sum(part[0] + part[1], axis=1, keepdims=True)
     reward = reward[0:steps] + reward[steps : 2 * steps]

time: 30.1 us -> 29.4 us (0.977)
  the two profiles are of different devices: /device:TPU:29 before, /device:TPU:0 now
where the time goes in v4:
time: 29.4 us; the launch traced here: 29.2 us
  Pallas kernels  23.5 us (80%)
  between operations  4.34 us (15%)
  local copies, waits for them, and re-layouts  1.39 us (5%)
    pallas_call x1, Pallas kernels, per_device(): pl.pallas_call(functools.partial(kernel, n), out_shape=(jax.ShapeDtypeStr...  23.5 us
    unnamed x1, local copies, waits for them, and re-layouts  1.39 us

profile of v4, /device:TPU:0, one launch (start us, length us, event | category | flops | bytes accessed | tf_op | source)
XLA Modules:
  0.0 29.2 jit_solution(1280742448669224680)
XLA Ops:
  2.6 23.5 %shard_map.104 = (bf16[1,4,4096]{2,1,0:T(4,128)(2,1)}, f32[1]{0:T(128)}) custom-call(s32[1]{0:T(128)S(6)} %copy.13.lengths_in, f32[1]{0:T(128)S(6)} %copy.14.parent_scores_in, s32[1]{0:T(128)S(6)} %copy.15.parents_in, bf16[1,4,4096]{2,1,0:T(4,128)(2,1)} %queries_in.1, bf16[1,4,512]{2,1,0:T(4,128)(2,1)} %new_keys_in.1, bf16[1,4,512]{2,1,0:T(4,128)(2,1)} %new_values_in.1, ...), custom_call_target="tpu_custom_call" | custom-call | tf_op jit(solution)/shard_map/pallas_call | solution.py:399
  26.1 1.4 %copy.16 = bf16[1,4,4096]{2,1,0:T(4,128)(2,1)} copy(bf16[1,4,4096]{2,1,0:T(4,128)(2,1)} %get-tuple-element.4) | data formatting | bytes 65536

commit v5 on v4

--- a/solution.py
+++ b/solution.py
@@ -19,6 +19,14 @@
     while n % (2 * inner) == 0 and 4 * inner * inner <= n:
         inner *= 2
     return inner
+
+
+def each_peer(n, body):
+    if n <= 16:
+        for k in range(n - 1):
+            body(k, 0)
+    else:
+        lax.fori_loop(0, n - 1, body, 0)
 
 
 def kernel(
@@ -100,13 +108,13 @@
     barrier = pltpu.get_barrier_semaphore()
 
     def peer(k):
-        return lax.rem(me + 1 + k, n)
+        return jnp.where(me + 1 + k >= n, me + 1 + k - n, me + 1 + k)
 
     def greet(k, carry):
         pl.semaphore_signal(barrier, inc=1, device_id={"dp": peer(k)}, device_id_type=MESH)
         return carry
 
-    lax.fori_loop(0, n - 1, greet, 0)
+    each_peer(n, greet)
     pl.semaphore_signal(barrier, inc=1, device_id={"tensor": 1 - core}, device_id_type=MESH)
 
     small[0].wait()
@@ -188,7 +196,7 @@
 
     lax.fori_loop(0, outer - 1, ask_far, 0)
     ask_near(z, True)
-    lax.fori_loop(0, n - 1, tell, 0)
+    each_peer(n, tell)
 
     for copy in small[2:]:
         copy.wait()
@@ -246,7 +254,7 @@
         ask_copy(slot, me, me).wait_recv()
         return carry
 
-    lax.fori_loop(0, n - 1, asked_wait, 0)
+    each_peer(n, asked_wait)
     lax.fori_loop(0, outer * (inner - 1), passed_wait, 0)
 
     def find(slot, carry):
@@ -258,7 +266,11 @@
         )
 
     first, last = lax.fori_loop(
-        0, n, find, (jnp.full((8, HD), n, jnp.int32), jnp.full((8, HD), -1, jnp.int32))
+        0,
+        n,
+        find,
+        (jnp.full((8, HD), n, jnp.int32), jnp.full((8, HD), -1, jnp.int32)),
+        unroll=n <= 16,
     )
     first = jnp.minimum(jnp.max(first), n - 1)
     last = jnp.maximum(jnp.max(last), 0)
@@ -309,7 +321,7 @@
         lse_copy(me, to).start()
         return carry
 
-    lax.fori_loop(0, n - 1, reply, 0)
+    each_peer(n, reply)
     got[me] = jnp.where(me == first, out_by_child[0], out_by_child[1])
     got_lse[me, 0:1, :] = jnp.where(me == first, lse_by_child[0], lse_by_child[1])
     got_lse[me, 1:2, :] = score_row
@@ -319,7 +331,7 @@
         lse_copy(peer(k), me).wait_recv()
         return carry
 
-    lax.fori_loop(0, n - 1, reply_wait, 0)
+    each_peer(n, reply_wait)
 
     holder = parents[0]
     parent_out = got[holder].astype(F32)
@@ -368,7 +380,7 @@
         ask_near(k, False)
         return carry
 
-    lax.fori_loop(0, n - 1, sent_wait, 0)
+    each_peer(n, sent_wait)
     lax.fori_loop(0, outer - 1, far_wait, 0)
     lax.fori_loop(0, outer, near_wait, 0)
     part_copy.wait()

time: 29.4 us -> 29.4 us (level)
  no operation moved by 1% of the time
where the time goes in v5:
time: 29.4 us; the launch traced here: 29.2 us
  Pallas kernels  23.4 us (80%)
  between operations  4.34 us (15%)
  local copies, waits for them, and re-layouts  1.39 us (5%)
    pallas_call x1, Pallas kernels, per_device(): pl.pallas_call(functools.partial(kernel, n), out_shape=(jax.ShapeDtypeStr...  23.4 us
    unnamed x1, local copies, waits for them, and re-layouts  1.39 us

profile of v5, /device:TPU:0, one launch (start us, length us, event | category | flops | bytes accessed | tf_op | source)
XLA Modules:
  0.0 29.2 jit_solution(14364306157503846179)
XLA Ops:
  2.6 23.4 %shard_map.104 = (bf16[1,4,4096]{2,1,0:T(4,128)(2,1)}, f32[1]{0:T(128)}) custom-call(s32[1]{0:T(128)S(6)} %copy.13.lengths_in, f32[1]{0:T(128)S(6)} %copy.14.parent_scores_in, s32[1]{0:T(128)S(6)} %copy.15.parents_in, bf16[1,4,4096]{2,1,0:T(4,128)(2,1)} %queries_in.1, bf16[1,4,512]{2,1,0:T(4,128)(2,1)} %new_keys_in.1, bf16[1,4,512]{2,1,0:T(4,128)(2,1)} %new_values_in.1, ...), custom_call_target="tpu_custom_call" | custom-call | tf_op jit(solution)/shard_map/pallas_call | solution.py:411
  26.0 1.4 %copy.16 = bf16[1,4,4096]{2,1,0:T(4,128)(2,1)} copy(bf16[1,4,4096]{2,1,0:T(4,128)(2,1)} %get-tuple-element.4) | data formatting | bytes 65536
